TPU v7x, 32 devices: a whole 2x2x4 slice. The times are simulated.
32 devices in a mesh: grp: 2 (over x), pb: 8 (over z, y), row: 2 (over core).
Axes of the slice: x: 2, y: 2, z: 4, core: 2. Of those that a mesh axis runs over, the one named last changes fastest.
Arguments:
- record: float32 [4096, 1024], P(('grp', 'pb', 'row')), parts along dimension 0, may hold values from -12 to 12
- record_tail: float32 [254, 1024], P('grp'), parts along dimension 0, may hold values from -12 to 12
- projection: float32 [1024, 16], replicated, may hold values from -0.1875 to 0.1875
- window_start: int32 [2], P('grp'), parts along dimension 0, may hold values from 0 to 64
Outputs:
- row_profile: float32 [4096], P(('grp', 'pb', 'row')), parts along dimension 0
- col_profile: float32 [4096], P(('grp', 'pb', 'row')), parts along dimension 0
There are 2 independent parts, one for each index of `grp`. A program takes and returns all parts, laid end to end along the dimension named above; an argument that names none is the same for every part. Nothing has to cross between parts.
All inputs are finite; a program needn't handle non-finite values.
Results may differ from a plain program's by a relative error of at most 0.0003.
Values sent between devices are 32-bit elements; how exact they have to be, the bound alone decides.
A program may use at most 64 MiB of HBM per device.

v0:
```python
import math

import jax
import jax.numpy as jnp
from jax import lax
from jax.sharding import PartitionSpec as P

M = 64


epsilon = 1e-05
ceiling = 4.0
group_limit = 8


def shifted(shard, axis, by):
    devices = lax.axis_size(axis)
    pairs = [(i, i + by) for i in range(devices) if 0 <= i + by < devices]
    return lax.ppermute(shard, axis, pairs)


def zscores(window, count_rows):
    hankel = jnp.stack(
        [window[..., offset : offset + count_rows, :] for offset in range(M)], axis=-2
    )
    center = jnp.mean(hankel, axis=-2, keepdims=True)
    spread = jnp.mean(jnp.square(hankel - center), axis=-2, keepdims=True)
    scaled = (
        (hankel - center) * lax.rsqrt(spread + epsilon) * (1.0 / math.sqrt(M * hankel.shape[-1]))
    )
    return scaled.astype(jnp.bfloat16)


def block_wanted(member_blocks):
    return member_blocks >= 0


def sweep(profile, windows, own_scores, me_index):
    count_blocks = windows.shape[0]
    row_count = own_scores.shape[0]
    group_size = min(group_limit, count_blocks)
    turns = -(-count_blocks // group_size)
    exclusion = M // 4
    row_index = me_index * row_count + jnp.arange(row_count, dtype=jnp.int32)

    def one_group(turn_index, current):
        local_first = jnp.minimum(turn_index * group_size, count_blocks - group_size).astype(
            jnp.int32
        )
        member_blocks = local_first + jnp.arange(group_size, dtype=jnp.int32)
        member_used = block_wanted(member_blocks)
        wanted = jnp.any(member_used)

        def compute_group(current_state):
            chosen = lax.dynamic_slice_in_dim(windows, local_first, group_size, 0)
            other_scores = zscores(chosen, row_count).reshape(group_size * row_count, -1)
            product = lax.dot_general(
                own_scores,
                other_scores,
                (((1,), (1,)), ((), ())),
                preferred_element_type=jnp.float32,
            )
            distance = 2.0 - 2.0 * product
            column_index = local_first * row_count + jnp.arange(
                group_size * row_count, dtype=jnp.int32
            )
            column_used = jnp.repeat(member_used, row_count)[None, :]
            separation = column_index[None, :] - row_index[:, None]
            after_vals = jnp.where((separation > exclusion) & column_used, distance, ceiling)
            before_vals = jnp.where((separation < -exclusion) & column_used, distance, ceiling)
            own_part = jnp.stack(
                [jnp.min(after_vals, axis=1), jnp.min(before_vals, axis=1)], axis=0
            )[None]
            old_own = lax.dynamic_slice_in_dim(current_state, me_index, 1, 0)
            return lax.dynamic_update_slice_in_dim(
                current_state, jnp.minimum(old_own, own_part), me_index, 0
            )

        def keep_group(current_state):
            return current_state

        return lax.cond(wanted, compute_group, keep_group, current)

    return lax.fori_loop(0, turns, one_group, profile)


def per_device(record, record_tail, projection, window_start):
    row_count = record.shape[0]
    blocks = lax.axis_size("pb") * lax.axis_size("row")
    me_index = lax.axis_index("pb") * lax.axis_size("row") + lax.axis_index("row")
    start_row = window_start[0]
    window_rows = row_count + M - 1
    projected = jnp.dot(
        record, projection, precision=lax.Precision.HIGHEST, preferred_element_type=jnp.float32
    )
    tail_projected = jnp.dot(
        record_tail, projection, precision=lax.Precision.HIGHEST, preferred_element_type=jnp.float32
    )
    initial = jnp.full((blocks, 2, row_count), ceiling, jnp.float32)
    head_rows = record_tail.shape[0]
    following = shifted(projected[:head_rows], ("pb", "row"), -1)
    following = jnp.where(me_index == blocks - 1, tail_projected, following)
    joined = jnp.concatenate([projected, following], axis=0)
    window = lax.dynamic_slice_in_dim(joined, start_row, window_rows, 0)
    own_scores = zscores(window, row_count).reshape(row_count, -1)
    profile = sweep(
        initial,
        lax.all_gather(window[None], ("pb", "row"), axis=0, tiled=True),
        own_scores,
        me_index,
    )
    final = lax.dynamic_index_in_dim(profile, me_index, 0, keepdims=False)
    return (final[0], final[1])


def solution(mesh):
    return jax.shard_map(
        per_device,
        mesh=mesh,
        in_specs=(P(("grp", "pb", "row"), None), P("grp", None), P(), P("grp")),
        out_specs=(P(("grp", "pb", "row")), P(("grp", "pb", "row"))),
        check_vma=False,
    )
```

profile of v0, /device:TPU:0, one launch (start us, length us, event | category | flops | bytes accessed | tf_op | source)
XLA Modules:
  0.0 141.3 jit_solution(16936125335749751949)
XLA Ops:
  0.6 1.0 copy-done
  1.7 1.4 fusion.18
  3.0 1.3 collective-permute-start
  5.0 1.1 collective-permute-done
  6.1 1.6 %convolution_select_fusion = f32[127,16]{0,1:T(8,128)S(1)} fusion(f32[127,16]{0,1:T(8,128)S(1)} %collective-permute-done, f32[127,1024]{1,0:T(8,128)} %param.9, f32[1024,16]{0,1:T(8,128)} %param.10, pred[]{:T(512)S(6)} %eq.3), kind=kOutput, calls=%fused_computation.90 | convolution fusion | flops 24971248 | bytes 601985 | tf_op jit(solution)/shard_map/dot_general | solution.py:96
  13.0 24.0 %all-gather.1 = f32[16,191,16]{1,2,0:T(8,128)S(1)} all-gather(f32[1,191,16]{1,2,0:T(8,128)S(1)} %bitcast.297), channel_id=2, replica_groups=mesh['grp'=2,'pb'=8,'row'=2] {'pb','row'}, dimensions={0}, use_global_device_ids=true | all-gather | bytes 207808 | tf_op jit(solution)/shard_map/all_gather | solution.py:108
  37.2 103.6 %while.17 = (s32[]{:T(128)}, f32[16,2,128]{2,1,0:T(2,128)S(1)}, s32[]{:T(128)}, f32[16,191,16]{1,0,2:T(8,128)S(1)}, bf16[128,1024]{1,0:T(8,128)(2,1)S(1)}, /*index=5*/s32[]{:T(128)}, s32[]{:T(128)}, s32[]{:T(128)}) while((s32[]{:T(128)}, f32[16,2,128]{2,1,0:T(2,128)S(1)}, s32[]{:T(128)}, f32[16,191,16]{1,0,2:T(8,128)S(1)}, ...), condition=%wide.region_8.0_spmd.clone, body=%wide.region_1.8_spmd.clone.sunk | while | flops 278283744 | bytes 42682168 | solution.py:84
  38.6 50.4 %conditional.3 = (f32[16,2,128]{2,1,0:T(2,128)S(1)}) conditional(s32[]{:T(128)} %convert_element_type.27, f32[16,2,128]{2,1,0:T(2,128)S(1)} %get-tuple-element.245, (s32[]{:T(128)}, f32[16,2,128]{2,1,0:T(2,128)S(1)}, s32[]{:T(128)}, s32[]{:T(128)}, pred[8]{0:T(512)(128)(4,1)S(1)}, /*index=5*/f32[16,191,16]{1,0,2:T(8,128)S(1)}, ...), branch_computations={%region_3.3_spmd, %region_4.7_spmd} | conditional | flops 278283712 | bytes 42681464 | solution.py:82
  42.1 0.7 constant_dynamic-update-slice_fusion.58
  49.2 0.7 constant_dynamic-update-slice_fusion.48
  69.1 0.7 constant_dynamic-update-slice_fusion.20
  71.2 0.7 constant_dynamic-update-slice_fusion.17
  79.8 0.7 constant_dynamic-update-slice_fusion.5
  84.0 2.1 %add_multiply_fusion = f32[8,128,16]{1,0,2:T(8,128)S(1)} fusion(f32[16,191,16]{1,0,2:T(8,128)S(1)} %get-tuple-element.128, s32[]{:T(128)S(6)} %select_n.22, s32[]{:T(128)S(6)} %add.164, s32[]{:T(128)S(6)} %add.163, s32[]{:T(128)S(6)} %add.162, s32[]{:T(128)S(6)} %add.161, s32[]{:T(128)S(6)} %add.160, s32[]{:T(128)S(6)} %add.159, s32[]{:T(128)S(6)} %add.158, ...), kind=kLoop, calls=%fused_computation.80 | loop fusion | flops 1048576 | bytes 4260096 | tf_op jit(solution)/shard_map/while/body/eval_jaxpr/cond/branch_1_fun/div | solution.py:26
  86.8 0.7 multiply_convert_fusion
  87.6 1.3 select_reduce_fusion.1
  90.4 50.4 %conditional.3 = (f32[16,2,128]{2,1,0:T(2,128)S(1)}) conditional(s32[]{:T(128)} %convert_element_type.27, f32[16,2,128]{2,1,0:T(2,128)S(1)} %get-tuple-element.245, (s32[]{:T(128)}, f32[16,2,128]{2,1,0:T(2,128)S(1)}, s32[]{:T(128)}, s32[]{:T(128)}, pred[8]{0:T(512)(128)(4,1)S(1)}, /*index=5*/f32[16,191,16]{1,0,2:T(8,128)S(1)}, ...), branch_computations={%region_3.3_spmd, %region_4.7_spmd} | conditional | flops 278283712 | bytes 42681464 | solution.py:82
  93.9 0.7 constant_dynamic-update-slice_fusion.58
  101.0 0.7 constant_dynamic-update-slice_fusion.48
  120.9 0.7 constant_dynamic-update-slice_fusion.20
  131.5 0.7 constant_dynamic-update-slice_fusion.5
  135.8 2.2 %add_multiply_fusion = f32[8,128,16]{1,0,2:T(8,128)S(1)} fusion(f32[16,191,16]{1,0,2:T(8,128)S(1)} %get-tuple-element.128, s32[]{:T(128)S(6)} %select_n.22, s32[]{:T(128)S(6)} %add.164, s32[]{:T(128)S(6)} %add.163, s32[]{:T(128)S(6)} %add.162, s32[]{:T(128)S(6)} %add.161, s32[]{:T(128)S(6)} %add.160, s32[]{:T(128)S(6)} %add.159, s32[]{:T(128)S(6)} %add.158, ...), kind=kLoop, calls=%fused_computation.80 | loop fusion | flops 1048576 | bytes 4260096 | tf_op jit(solution)/shard_map/while/body/eval_jaxpr/cond/branch_1_fun/div | solution.py:26
  138.6 0.7 multiply_convert_fusion
  139.4 1.3 select_reduce_fusion.1
  (214 shorter events, 93.0 us)
Async XLA Ops:
  0.6 1.0 copy-start
  3.0 3.1 %collective-permute-start = (f32[127,16]{0,1:T(8,128)S(1)}, f32[127,16]{0,1:T(8,128)S(1)}, u32[]{:S(2)}, u32[]{:S(2)}) collective-permute-start(f32[127,16]{0,1:T(8,128)S(1)} %bitcast.300), channel_id=1, source_target_pairs={{1,0},{2,1},{3,2},{4,3},{5,4},{6,5},{7,6},{8,7},{9,8},{10,9},{11,1... | collective-permute-start | bytes 24392 | tf_op jit(solution)/shard_map/ppermute | solution.py:19
  84.0 2.2 %copy-start.1 = (f32[8,128,64,16]{1,0,3,2:T(8,128)S(1)}, f32[8,128,64,16]{1,0,3,2:T(8,128)}, u32[]{:S(2)}) copy-start(f32[8,128,64,16]{1,0,3,2:T(8,128)} %constant_dynamic-update-slice_fusion) | copy-start | bytes 12582916 | tf_op jit(solution)/shard_map/while/body/eval_jaxpr/cond
  135.8 2.2 %copy-start.1 = (f32[8,128,64,16]{1,0,3,2:T(8,128)S(1)}, f32[8,128,64,16]{1,0,3,2:T(8,128)}, u32[]{:S(2)}) copy-start(f32[8,128,64,16]{1,0,3,2:T(8,128)} %constant_dynamic-update-slice_fusion) | copy-start | bytes 12582916 | tf_op jit(solution)/shard_map/while/body/eval_jaxpr/cond
where the time goes:
time: 142 us; the launch traced here: 141 us
  local copies, waits for them, and re-layouts  97.4 us (69%)
  blocking collectives  24 us (17%)
  other arithmetic  8.86 us (6%)
  matrix products  5.58 us (4%)
  loops' own time  1.63 us (1%)
    cond x130, local copies, waits for them, and re-layouts  89.4 us
    all_gather x1, blocking collectives, per_device(): lax.all_gather(window[None], ('pb', 'row'), axis=0, tiled=True)  24 us
    unnamed x67, local copies, waits for them, and re-layouts  5.85 us
    div x3, other arithmetic, zscores(): center = jnp.mean(hankel, axis=-2, keepdims=True)  4.51 us
  transfers between devices with their start and end apart: 1, of which 1 were waited for; matrix products, arithmetic and copies ran while one was open for 0% of the time, Pallas kernels for 0%

commit v1 on v0

v1 whole, which is shorter than its diff:
```python
import functools
import math

import jax
import jax.numpy as jnp
from jax import lax
from jax.experimental import pallas as pl
from jax.experimental.pallas import tpu as pltpu
from jax.sharding import PartitionSpec as P

M = 64
LANES = 128
epsilon = 1e-05
MESH = pl.DeviceIdType.MESH
NT = (((1,), (1,)), ((), ()))


def kernel(
    blocks,
    row_devices,
    start_ref,
    record_hbm,
    tail_hbm,
    projection_ref,
    later_ref,
    earlier_ref,
    record_ref,
    tail_ref,
    spaced_ref,
    packed_ref,
    hankel_ref,
    own_ref,
    chunk_ref,
    load_sems,
    send_sems,
    recv_sems,
):
    rows = record_ref.shape[0]
    head_rows = tail_ref.shape[0]
    dims = projection_ref.shape[0]
    steps = LANES // dims
    packed_rows = rows // steps
    exclusion = M // 4
    pb_index = lax.axis_index("pb")
    row_index = lax.axis_index("row")
    me = pb_index * row_devices + row_index

    def place(block):
        return {"pb": lax.div(block, row_devices), "row": lax.rem(block, row_devices)}

    def peer_of(distance):
        return lax.rem(me + distance, blocks)

    def slot(block):
        return packed_ref.at[pl.ds(pl.multiple_of(block * packed_rows, packed_rows), packed_rows)]

    def block_copy(source, target, distance):
        return pltpu.make_async_remote_copy(
            src_ref=slot(source),
            dst_ref=slot(source),
            send_sem=send_sems.at[distance],
            recv_sem=recv_sems.at[source],
            device_id=place(target),
            device_id_type=MESH,
        )

    record_copy = pltpu.make_async_copy(record_hbm, record_ref, load_sems.at[0])
    record_copy.start()
    tail_copy = pltpu.make_async_copy(tail_hbm, tail_ref, load_sems.at[1])
    tail_copy.start()

    barrier = pltpu.get_barrier_semaphore()

    def greet(distance, carry):
        pl.semaphore_signal(
            barrier, inc=1, device_id=place(peer_of(distance)), device_id_type=MESH
        )
        return carry

    lax.fori_loop(1, blocks, greet, 0)

    repeated = jnp.concatenate([projection_ref[...]] * steps, axis=0)
    group = lax.broadcasted_iota(jnp.int32, (steps, LANES), 1) // dims
    row_in_group = lax.broadcasted_iota(jnp.int32, (steps, LANES), 0)
    keep = (group == row_in_group)[None]

    def pack(values):
        split = values.reshape(values.shape[0] // steps, steps, LANES)
        return jnp.sum(jnp.where(keep, split, 0.0), axis=1)

    record_copy.wait()
    projected = lax.dot_general(
        record_ref[...], repeated, NT,
        precision=lax.Precision.HIGHEST, preferred_element_type=jnp.float32,
    )
    slot(me)[...] = pack(projected)

    pl.semaphore_wait(barrier, blocks - 1)

    def send(distance, carry):
        block_copy(me, peer_of(distance), distance).start()
        return carry

    lax.fori_loop(1, blocks, send, 0)

    tail_copy.wait()
    spaced_ref[...] = jnp.zeros_like(spaced_ref)
    spaced_ref[pl.ds(0, head_rows), :] = lax.dot_general(
        tail_ref[...], repeated, NT,
        precision=lax.Precision.HIGHEST, preferred_element_type=jnp.float32,
    )
    tail_base = blocks * packed_rows
    packed_ref[pl.ds(tail_base, packed_rows), :] = pack(spaced_ref[...])
    packed_ref[pl.ds(tail_base + packed_rows, 8), :] = jnp.zeros((8, LANES), jnp.float32)

    def arrive(distance, carry):
        block_copy(peer_of(distance), me, distance).wait_recv()
        return carry

    lax.fori_loop(1, blocks, arrive, 0)

    lane = lax.broadcasted_iota(jnp.int32, (packed_rows, LANES), 1)

    def expand(block, carry):
        base = pl.multiple_of(block * packed_rows, packed_rows)
        here = packed_ref[pl.ds(base, packed_rows), :]
        after = packed_ref[pl.ds(base + 1, packed_rows), :]
        out = pl.multiple_of(block * rows, rows)
        for step in range(steps):
            if step == 0:
                moved = here
            else:
                mixed = jnp.where(lane >= step * dims, here, after)
                moved = pltpu.roll(mixed, LANES - step * dims, 1)
            hankel_ref[pl.ds(out + step, packed_rows, stride=steps), :] = moved
        return carry

    lax.fori_loop(0, blocks + 1, expand, 0, unroll=1)

    start = start_ref[0]
    turns = M // steps

    def all_steps(values):
        shift = LANES // 2
        while shift >= dims:
            values = values + pltpu.roll(values, shift, 1)
            shift //= 2
        return values

    def scores(block, out_ref, out_row):
        span = rows + M - steps
        held = hankel_ref[pl.ds(block * rows + start, span), :]
        total, reach, have = held, steps, 1
        while have < turns:
            total = total[: total.shape[0] - reach] + total[reach:]
            reach, have = reach * 2, have * 2
        center = all_steps(total[:rows]) * (1.0 / M)
        parts = [held[turn * steps : turn * steps + rows] - center for turn in range(turns)]
        square = parts[0] * parts[0]
        for part in parts[1:]:
            square = square + part * part
        spread = all_steps(square) * (1.0 / M)
        scale = lax.rsqrt(spread + epsilon) * (1.0 / math.sqrt(M * dims))
        for turn, part in enumerate(parts):
            out_ref[pl.ds(out_row, rows), pl.ds(turn * LANES, LANES)] = (part * scale).astype(
                jnp.bfloat16
            )

    scores(me, own_ref, 0)
    own = own_ref[...]
    chunk_blocks = chunk_ref.shape[0] // rows
    chunk_rows = chunk_ref.shape[0]
    offset = lax.broadcasted_iota(jnp.int32, (chunk_rows, rows), 0) - lax.broadcasted_iota(
        jnp.int32, (chunk_rows, rows), 1
    )

    def one_chunk(chunk, carry):
        later, earlier = carry
        for part in range(chunk_blocks):
            scores(chunk * chunk_blocks + part, chunk_ref, part * rows)
        product = lax.dot_general(
            chunk_ref[...], own, NT, preferred_element_type=jnp.float32
        )
        separation = offset + (chunk * chunk_rows - me * rows)
        after = jnp.where(separation > exclusion, product, -1.0)
        before = jnp.where(separation < -exclusion, product, -1.0)
        after = jnp.max(after.reshape(chunk_rows // 8, 8, rows), axis=0)
        before = jnp.max(before.reshape(chunk_rows // 8, 8, rows), axis=0)
        return jnp.maximum(later, after), jnp.maximum(earlier, before)

    low = jnp.full((8, rows), -1.0, jnp.float32)
    later, earlier = lax.fori_loop(0, blocks // chunk_blocks, one_chunk, (low, low))
    later_ref[...] = 2.0 - 2.0 * jnp.max(later, axis=0, keepdims=True)
    earlier_ref[...] = 2.0 - 2.0 * jnp.max(earlier, axis=0, keepdims=True)

    def sent(distance, carry):
        block_copy(me, peer_of(distance), distance).wait_send()
        return carry

    lax.fori_loop(1, blocks, sent, 0)


def per_device(record, record_tail, projection, window_start):
    rows, channels = record.shape
    head_rows = record_tail.shape[0]
    dims = projection.shape[1]
    row_devices = lax.axis_size("row")
    blocks = lax.axis_size("pb") * row_devices
    steps = LANES // dims
    packed_rows = rows // steps
    chunk_blocks = math.gcd(4, blocks)
    vmem = pl.BlockSpec(memory_space=pltpu.VMEM)
    hbm = pl.BlockSpec(memory_space=pl.ANY)
    f32 = jnp.float32
    later, earlier = pl.pallas_call(
        functools.partial(kernel, blocks, row_devices),
        out_shape=[jax.ShapeDtypeStruct((1, rows), f32)] * 2,
        in_specs=[pl.BlockSpec(memory_space=pltpu.SMEM), hbm, hbm, vmem],
        out_specs=[vmem, vmem],
        scratch_shapes=[
            pltpu.VMEM((rows, channels), f32),
            pltpu.VMEM((head_rows, channels), f32),
            pltpu.VMEM((rows, LANES), f32),
            pltpu.VMEM(((blocks + 1) * packed_rows + 8, LANES), f32),
            pltpu.VMEM(((blocks + 1) * rows, LANES), f32),
            pltpu.VMEM((rows, M * dims), jnp.bfloat16),
            pltpu.VMEM((chunk_blocks * rows, M * dims), jnp.bfloat16),
            pltpu.SemaphoreType.DMA((2,)),
            pltpu.SemaphoreType.DMA((blocks,)),
            pltpu.SemaphoreType.DMA((blocks,)),
        ],
        compiler_params=pltpu.CompilerParams(
            collective_id=0, has_side_effects=True, vmem_limit_bytes=40 * 1024 * 1024
        ),
    )(window_start, record, record_tail, projection.T)
    return later.reshape(rows), earlier.reshape(rows)


def solution(mesh):
    return jax.shard_map(
        per_device,
        mesh=mesh,
        in_specs=(P(("grp", "pb", "row"), None), P("grp", None), P(), P("grp")),
        out_specs=(P(("grp", "pb", "row")), P(("grp", "pb", "row"))),
        check_vma=False,
    )
```

time: 142 us -> 22.1 us (0.16)
  local copies, waits for them, and re-layouts: 97.4 us -> 3.94 us
  blocking collectives: 24 us -> 0 us
  Pallas kernels: 0 us -> 16.6 us
  other arithmetic: 8.86 us -> 0 us
  matrix products: 5.58 us -> 0 us
  loops' own time: 1.63 us -> 0 us
    cond x130 -> x0, local copies, waits for them, and re-layouts: 89.4 us -> none
    all_gather x1 -> x0, blocking collectives: 24 us -> none  [per_device(): lax.all_gather(window[None], ('pb', 'row'), axis=0, tiled=True)]
    pallas_call x0 -> x1, Pallas kernels: none -> 16.6 us  [per_device(): pl.pallas_call(functools.partial(kernel, blocks, row_devices), out_shape=...]
    dot_general x4 -> x0, matrix products: 5.58 us -> none  [the longest x2 2.68 us: compute_group(): lax.dot_general(own_scores, other_scores, (((1,), (1,)), ((), ())), prefe...]
    div x3 -> x0, other arithmetic: 4.51 us -> none  [zscores(): center = jnp.mean(hankel, axis=-2, keepdims=True)]
    unnamed x67 -> x8, local copies, waits for them, and re-layouts: 5.85 us -> 3.94 us
    another operation x3 -> x0, loops' own time: 1.63 us -> none  [the longest x1 1.44 us: sweep(): return lax.fori_loop(0, turns, one_group, profile)]
    convert_element_type x3 -> x0, other arithmetic: 1.52 us -> none  [zscores(): return scaled.astype(jnp.bfloat16)]
  transfers between devices with their start and end apart: 1 -> 0, of which waited for: 1 -> 0; matrix products, arithmetic and copies ran while one was open for 0% -> 0% of each run, Pallas kernels for 0% -> 0%
where the time goes in v1:
time: 22.1 us; the launch traced here: 21.8 us
  Pallas kernels  16.6 us (75%)
  local copies, waits for them, and re-layouts  3.94 us (18%)
  between operations  1.3 us (6%)
    pallas_call x1, Pallas kernels, per_device(): pl.pallas_call(functools.partial(kernel, blocks, row_devices), out_shape=...  16.6 us
    unnamed x8, local copies, waits for them, and re-layouts  3.94 us

profile of v1, /device:TPU:0, one launch (start us, length us, event | category | flops | bytes accessed | tf_op | source)
XLA Modules:
  0.0 21.8 jit_solution(3497634450893240470)
XLA Ops:
  1.3 0.0 copy-start
  1.3 1.0 %copy-done = f32[128,1024]{1,0:T(8,128)S(1)} copy-done((f32[128,1024]{1,0:T(8,128)S(1)}, f32[128,1024]{1,0:T(8,128)}, u32[]{:S(2)}) %copy-start) | copy-done | bytes 524312
  2.3 0.0 copy-start.1
  2.3 1.0 %copy-done.1 = f32[127,1024]{1,0:T(8,128)S(1)} copy-done((f32[127,1024]{1,0:T(8,128)S(1)}, f32[127,1024]{1,0:T(8,128)}, u32[]{:S(2)}) %copy-start.1) | copy-done | bytes 520216
  3.4 0.0 copy-start.2
  3.4 0.8 %copy-done.2 = f32[1024,16]{0,1:T(8,128)S(1)} copy-done((f32[1024,16]{0,1:T(8,128)S(1)}, f32[1024,16]{0,1:T(8,128)}, u32[]{:S(2)}) %copy-start.2) | copy-done | bytes 65560
  4.2 16.6 %shard_map.59 = (f32[1,128]{1,0:T(1,128)S(1)}, f32[1,128]{1,0:T(1,128)S(1)}) custom-call(s32[1]{0:T(128)S(6)} %copy.8.start_ref, f32[128,1024]{1,0:T(8,128)S(1)} %copy-done, f32[127,1024]{1,0:T(8,128)S(1)} %copy-done.1, f32[16,1024]{1,0:T(8,128)S(1)} %bitcast.3), custom_call_target="tpu_custom_call" | custom-call | tf_op jit(solution)/shard_map/pallas_call | solution.py:215
  20.8 0.5 %copy.9 = f32[128]{0:T(128)} copy(f32[128]{0:T(128)S(1)} %bitcast.5) | data formatting | bytes 1024
  21.3 0.5 %copy.10 = f32[128]{0:T(128)} copy(f32[128]{0:T(128)S(1)} %bitcast.4) | data formatting | bytes 1024
Async XLA Ops:
  1.3 1.0 %copy-start = (f32[128,1024]{1,0:T(8,128)S(1)}, f32[128,1024]{1,0:T(8,128)}, u32[]{:S(2)}) copy-start(f32[128,1024]{1,0:T(8,128)} %record_hbm.1) | copy-start | bytes 1572868
  2.3 1.0 %copy-start.1 = (f32[127,1024]{1,0:T(8,128)S(1)}, f32[127,1024]{1,0:T(8,128)}, u32[]{:S(2)}) copy-start(f32[127,1024]{1,0:T(8,128)} %tail_hbm.1) | copy-start | bytes 1560580
  3.4 0.8 %copy-start.2 = (f32[1024,16]{0,1:T(8,128)S(1)}, f32[1024,16]{0,1:T(8,128)}, u32[]{:S(2)}) copy-start(f32[1024,16]{0,1:T(8,128)} %param.6) | copy-start | bytes 196612

commit v2 on v1

v2 whole, which is shorter than its diff:
```python
import functools
import math

import jax
import jax.numpy as jnp
from jax import lax
from jax.experimental import pallas as pl
from jax.experimental.pallas import tpu as pltpu
from jax.sharding import PartitionSpec as P

M = 64
LANES = 128
epsilon = 1e-05
MESH = pl.DeviceIdType.MESH
RECORD_COPIES = 4
NT = (((1,), (1,)), ((), ()))


def gather_kernel(
    blocks,
    row_devices,
    record_hbm,
    tail_hbm,
    projection_hbm,
    packed_ref,
    record_ref,
    tail_ref,
    projection_ref,
    spaced_ref,
    load_sems,
    send_sems,
    recv_sems,
):
    rows = record_ref.shape[0]
    head_rows = tail_ref.shape[0]
    dims = projection_ref.shape[0]
    steps = LANES // dims
    packed_rows = rows // steps
    pb_index = lax.axis_index("pb")
    row_index = lax.axis_index("row")
    me = pb_index * row_devices + row_index

    def place(block):
        return {"pb": lax.div(block, row_devices), "row": lax.rem(block, row_devices)}

    def peer_of(distance):
        return lax.rem(me + distance, blocks)

    def slot(block):
        return packed_ref.at[pl.ds(pl.multiple_of(block * packed_rows, packed_rows), packed_rows)]

    def block_copy(source, target, distance):
        return pltpu.make_async_remote_copy(
            src_ref=slot(source),
            dst_ref=slot(source),
            send_sem=send_sems.at[distance],
            recv_sem=recv_sems.at[source],
            device_id=place(target),
            device_id_type=MESH,
        )

    projection_copy = pltpu.make_async_copy(projection_hbm, projection_ref, load_sems.at[0])
    projection_copy.start()
    share = rows // RECORD_COPIES
    record_copies = [
        pltpu.make_async_copy(
            record_hbm.at[pl.ds(part * share, share)],
            record_ref.at[pl.ds(part * share, share)],
            load_sems.at[2 + part],
        )
        for part in range(RECORD_COPIES)
    ]
    for copy in record_copies:
        copy.start()
    tail_copy = pltpu.make_async_copy(tail_hbm, tail_ref, load_sems.at[1])
    tail_copy.start()

    barrier = pltpu.get_barrier_semaphore()

    def greet(distance, carry):
        pl.semaphore_signal(
            barrier, inc=1, device_id=place(peer_of(distance)), device_id_type=MESH
        )
        return carry

    lax.fori_loop(1, blocks, greet, 0)

    projection_copy.wait()
    repeated = jnp.concatenate([projection_ref[...]] * steps, axis=0)
    group = lax.broadcasted_iota(jnp.int32, (steps, LANES), 1) // dims
    row_in_group = lax.broadcasted_iota(jnp.int32, (steps, LANES), 0)
    keep = (group == row_in_group)[None]

    def pack(values):
        split = values.reshape(values.shape[0] // steps, steps, LANES)
        return jnp.sum(jnp.where(keep, split, 0.0), axis=1)

    for copy in record_copies:
        copy.wait()
    projected = lax.dot_general(
        record_ref[...], repeated, NT,
        precision=lax.Precision.HIGHEST, preferred_element_type=jnp.float32,
    )
    slot(me)[...] = pack(projected)

    pl.semaphore_wait(barrier, blocks - 1)

    def send(distance, carry):
        block_copy(me, peer_of(distance), distance).start()
        return carry

    lax.fori_loop(1, blocks, send, 0)

    tail_copy.wait()
    spaced_ref[...] = jnp.zeros_like(spaced_ref)
    spaced_ref[pl.ds(0, head_rows), :] = lax.dot_general(
        tail_ref[...], repeated, NT,
        precision=lax.Precision.HIGHEST, preferred_element_type=jnp.float32,
    )
    tail_base = blocks * packed_rows
    packed_ref[pl.ds(tail_base, packed_rows), :] = pack(spaced_ref[...])
    packed_ref[pl.ds(tail_base + packed_rows, 2 * steps), :] = jnp.zeros(
        (2 * steps, LANES), jnp.float32
    )

    def arrive(distance, carry):
        block_copy(peer_of(distance), me, distance).wait_recv()
        return carry

    lax.fori_loop(1, blocks, arrive, 0)

    def sent(distance, carry):
        block_copy(me, peer_of(distance), distance).wait_send()
        return carry

    lax.fori_loop(1, blocks, sent, 0)


def compute_kernel(
    blocks,
    row_devices,
    dims,
    start_ref,
    packed_ref,
    later_ref,
    earlier_ref,
    hankel_ref,
    center_ref,
    scale_ref,
    own_ref,
    chunk_ref,
):
    rows = own_ref.shape[0]
    steps = LANES // dims
    packed_rows = rows // steps
    tail_base = blocks * packed_rows
    exclusion = M // 4
    me = lax.axis_index("pb") * row_devices + lax.axis_index("row")

    picks = lax.broadcasted_iota(jnp.int32, (LANES, steps * LANES), 0)
    column = lax.broadcasted_iota(jnp.int32, (LANES, steps * LANES), 1)
    pick = (picks == column // LANES * dims + column % dims).astype(jnp.float32)
    pick = pick.astype(jnp.bfloat16)
    pick = jnp.concatenate([pick, pick, pick], axis=0)

    def later_steps(values, by):
        size = values.shape[0]
        if by >= steps:
            return pltpu.roll(values, size - by // steps, 0)
        lane = lax.broadcasted_iota(jnp.int32, values.shape, 1)
        mixed = jnp.where(lane >= by * dims, values, pltpu.roll(values, size - 1, 0))
        return pltpu.roll(mixed, LANES - by * dims, 1)

    def three_terms(values):
        high = values.astype(jnp.bfloat16)
        rest = values - high.astype(jnp.float32)
        middle = rest.astype(jnp.bfloat16)
        low = (rest - middle.astype(jnp.float32)).astype(jnp.bfloat16)
        return jnp.concatenate([high, middle, low], axis=1)

    def expand(base, count):
        held = packed_ref[pl.ds(base, count + 2 * steps), :]
        out = base * steps
        for step in range(steps):
            moved = held if step == 0 else later_steps(held, step)
            hankel_ref[pl.ds(out + step, count, stride=steps), :] = moved[:count]
        total = held
        square = jnp.zeros_like(held)
        have = 1
        while have < M:
            next_total = later_steps(total, have)
            if have > 1:
                square = square + later_steps(square, have)
            gap = total - next_total
            square = square + gap * gap * (0.5 / have)
            total = total + next_total
            have *= 2
        center = total[:count] * (1.0 / M)
        scale = lax.rsqrt(square[:count] * (1.0 / M) + epsilon) * (1.0 / math.sqrt(M * dims))
        for values, ref in ((center, center_ref), (scale, scale_ref)):
            spread_out = jnp.dot(
                three_terms(values), pick, preferred_element_type=jnp.float32
            )
            for step in range(steps):
                ref[pl.ds(out + step, count, stride=steps), :] = spread_out[
                    :, step * LANES : (step + 1) * LANES
                ]

    group_blocks = math.gcd(16, blocks)
    group_rows = group_blocks * packed_rows

    def expand_group(index, carry):
        expand(pl.multiple_of(index * group_rows, group_rows), group_rows)
        return carry

    if group_blocks == blocks:
        expand(0, tail_base + packed_rows)
    else:
        lax.fori_loop(0, blocks // group_blocks, expand_group, 0)
        expand(tail_base, packed_rows)

    start = start_ref[0]
    turns = M // steps
    piece = min(64, rows)

    def scores(first, out_ref, out_row):
        held = hankel_ref[pl.ds(first + start, piece + M - steps), :]
        center = center_ref[pl.ds(first + start, piece), :]
        scale = scale_ref[pl.ds(first + start, piece), :]
        for turn in range(turns):
            part = (held[turn * steps : turn * steps + piece] - center) * scale
            out_ref[pl.ds(out_row, piece), pl.ds(turn * LANES, LANES)] = part.astype(
                jnp.bfloat16
            )

    for part in range(rows // piece):
        scores(me * rows + part * piece, own_ref, part * piece)
    own = own_ref[...]
    chunk_rows = chunk_ref.shape[0]
    half = chunk_rows // 2
    offset = lax.broadcasted_iota(jnp.int32, (half, rows), 0) - lax.broadcasted_iota(
        jnp.int32, (half, rows), 1
    )

    def one_chunk(chunk, carry):
        later, earlier = carry
        for side in range(2):
            for part in range(half // piece):
                row = side * half + part * piece
                scores(chunk * chunk_rows + row, chunk_ref, row)
            product = lax.dot_general(
                chunk_ref[pl.ds(side * half, half), :], own, NT,
                preferred_element_type=jnp.float32,
            )
            separation = offset + (chunk * chunk_rows + side * half - me * rows)
            after = jnp.where(separation > exclusion, product, -1.0)
            before = jnp.where(separation < -exclusion, product, -1.0)
            after = jnp.max(after.reshape(half // 8, 8, rows), axis=0)
            before = jnp.max(before.reshape(half // 8, 8, rows), axis=0)
            later, earlier = jnp.maximum(later, after), jnp.maximum(earlier, before)
        return later, earlier

    chunk_blocks = chunk_rows // rows
    low = jnp.full((8, rows), -1.0, jnp.float32)
    later, earlier = lax.fori_loop(0, blocks // chunk_blocks, one_chunk, (low, low))
    later_ref[...] = 2.0 - 2.0 * jnp.max(later, axis=0, keepdims=True)
    earlier_ref[...] = 2.0 - 2.0 * jnp.max(earlier, axis=0, keepdims=True)


def per_device(record, record_tail, projection, window_start):
    rows, channels = record.shape
    head_rows = record_tail.shape[0]
    dims = projection.shape[1]
    row_devices = lax.axis_size("row")
    blocks = lax.axis_size("pb") * row_devices
    steps = LANES // dims
    packed_rows = rows // steps
    chunk_blocks = math.gcd(4, blocks)
    vmem = pl.BlockSpec(memory_space=pltpu.VMEM)
    hbm = pl.BlockSpec(memory_space=pltpu.HBM)
    f32 = jnp.float32
    packed = pl.pallas_call(
        functools.partial(gather_kernel, blocks, row_devices),
        out_shape=jax.ShapeDtypeStruct(((blocks + 1) * packed_rows + 2 * steps, LANES), f32),
        in_specs=[hbm, hbm, hbm],
        out_specs=vmem,
        scratch_shapes=[
            pltpu.VMEM((rows, channels), f32),
            pltpu.VMEM((head_rows, channels), f32),
            pltpu.VMEM((dims, channels), f32),
            pltpu.VMEM((rows, LANES), f32),
            pltpu.SemaphoreType.DMA((2 + RECORD_COPIES,)),
            pltpu.SemaphoreType.DMA((blocks,)),
            pltpu.SemaphoreType.DMA((blocks,)),
        ],
        compiler_params=pltpu.CompilerParams(
            collective_id=0, has_side_effects=True, vmem_limit_bytes=62 * 1024 * 1024
        ),
    )(record, record_tail, projection.T)
    later, earlier = pl.pallas_call(
        functools.partial(compute_kernel, blocks, row_devices, dims),
        out_shape=[jax.ShapeDtypeStruct((1, rows), f32)] * 2,
        in_specs=[pl.BlockSpec(memory_space=pltpu.SMEM), vmem],
        out_specs=[vmem, vmem],
        scratch_shapes=[pltpu.VMEM(((blocks + 1) * rows, LANES), f32)] * 3
        + [
            pltpu.VMEM((rows, M * dims), jnp.bfloat16),
            pltpu.VMEM((chunk_blocks * rows, M * dims), jnp.bfloat16),
        ],
        compiler_params=pltpu.CompilerParams(vmem_limit_bytes=48 * 1024 * 1024),
    )(window_start, packed)
    return later.reshape(rows), earlier.reshape(rows)


def solution(mesh):
    return jax.shard_map(
        per_device,
        mesh=mesh,
        in_specs=(P(("grp", "pb", "row"), None), P("grp", None), P(), P("grp")),
        out_specs=(P(("grp", "pb", "row")), P(("grp", "pb", "row"))),
        check_vma=False,
    )
```

time: 22.1 us -> 17.3 us (0.78)
  local copies, waits for them, and re-layouts: 3.94 us -> 0.9 us
  Pallas kernels: 16.6 us -> 15 us
    unnamed x8 -> x2, local copies, waits for them, and re-layouts: 3.94 us -> 0.9 us
    pallas_call x1 -> x2, Pallas kernels: 16.6 us -> 15 us  [the longest x1 10.9 us: per_device(): pl.pallas_call(functools.partial(gather_kernel, blocks, row_devices), out...]
where the time goes in v2:
time: 17.3 us; the launch traced here: 17.2 us
  Pallas kernels  15 us (87%)
  between operations  1.29 us (7%)
  local copies, waits for them, and re-layouts  0.9 us (5%)
    pallas_call x1, Pallas kernels, per_device(): pl.pallas_call(functools.partial(gather_kernel, blocks, row_devices), out...  10.9 us
    pallas_call x1, Pallas kernels, per_device(): pl.pallas_call(functools.partial(compute_kernel, blocks, row_devices, dim...  4.09 us
    unnamed x2, local copies, waits for them, and re-layouts  0.9 us

profile of v2, /device:TPU:0, one launch (start us, length us, event | category | flops | bytes accessed | tf_op | source)
XLA Modules:
  0.0 17.2 jit_solution(13480692678846184305)
XLA Ops:
  1.3 10.9 %shard_map.59.packed_ref = f32[288,128]{1,0:T(8,128)} custom-call(f32[128,1024]{1,0:T(8,128)} %record_hbm.1, f32[127,1024]{1,0:T(8,128)} %tail_hbm.1, f32[16,1024]{1,0:T(8,128)} %bitcast.3), custom_call_target="tpu_custom_call" | custom-call | tf_op jit(solution)/shard_map/pallas_call | solution.py:282
  12.2 0.0 copy-start
  12.2 0.9 %copy-done = f32[288,128]{1,0:T(8,128)S(1)} copy-done((f32[288,128]{1,0:T(8,128)S(1)}, f32[288,128]{1,0:T(8,128)}, u32[]{:S(2)}) %copy-start) | copy-done | bytes 147480
  13.1 4.1 %shard_map.60 = (f32[1,128]{1,0:T(1,128)}, f32[1,128]{1,0:T(1,128)}) custom-call(s32[1]{0:T(128)S(6)} %copy.6.start_ref, f32[288,128]{1,0:T(8,128)S(1)} %copy-done), custom_call_target="tpu_custom_call" | custom-call | tf_op jit(solution)/shard_map/pallas_call | solution.py:300
Async XLA Ops:
  12.2 0.9 %copy-start = (f32[288,128]{1,0:T(8,128)S(1)}, f32[288,128]{1,0:T(8,128)}, u32[]{:S(2)}) copy-start(f32[288,128]{1,0:T(8,128)} %shard_map.59.packed_ref) | copy-start | bytes 442372

commit v3 on v2

--- a/solution.py
+++ b/solution.py
@@ -16,17 +16,25 @@
 NT = (((1,), (1,)), ((), ()))
 
 
-def gather_kernel(
+def kernel(
     blocks,
     row_devices,
+    start_ref,
     record_hbm,
     tail_hbm,
     projection_hbm,
-    packed_ref,
+    best_ref,
     record_ref,
     tail_ref,
     projection_ref,
     spaced_ref,
+    packed_ref,
+    hankel_ref,
+    center_ref,
+    scale_ref,
+    own_ref,
+    chunk_ref,
+    pick_ref,
     load_sems,
     send_sems,
     recv_sems,
@@ -36,9 +44,11 @@
     dims = projection_ref.shape[0]
     steps = LANES // dims
     packed_rows = rows // steps
+    exclusion = M // 4
     pb_index = lax.axis_index("pb")
     row_index = lax.axis_index("row")
     me = pb_index * row_devices + row_index
+    unroll = blocks - 1 if blocks <= 16 else 1
 
     def place(block):
         return {"pb": lax.div(block, row_devices), "row": lax.rem(block, row_devices)}
@@ -83,7 +93,14 @@
         )
         return carry
 
-    lax.fori_loop(1, blocks, greet, 0)
+    lax.fori_loop(1, blocks, greet, 0, unroll=unroll)
+
+    picks = lax.broadcasted_iota(jnp.int32, (LANES, steps * LANES), 0)
+    column = lax.broadcasted_iota(jnp.int32, (LANES, steps * LANES), 1)
+    pick = (picks == column // LANES * dims + column % dims).astype(jnp.float32)
+    pick = pick.astype(jnp.bfloat16)
+    pick = jnp.concatenate([pick, pick, pick], axis=0)
+    pick_ref[...] = pick
 
     projection_copy.wait()
     repeated = jnp.concatenate([projection_ref[...]] * steps, axis=0)
@@ -109,7 +126,7 @@
         block_copy(me, peer_of(distance), distance).start()
         return carry
 
-    lax.fori_loop(1, blocks, send, 0)
+    lax.fori_loop(1, blocks, send, 0, unroll=unroll)
 
     tail_copy.wait()
     spaced_ref[...] = jnp.zeros_like(spaced_ref)
@@ -127,41 +144,7 @@
         block_copy(peer_of(distance), me, distance).wait_recv()
         return carry
 
-    lax.fori_loop(1, blocks, arrive, 0)
-
-    def sent(distance, carry):
-        block_copy(me, peer_of(distance), distance).wait_send()
-        return carry
-
-    lax.fori_loop(1, blocks, sent, 0)
-
-
-def compute_kernel(
-    blocks,
-    row_devices,
-    dims,
-    start_ref,
-    packed_ref,
-    later_ref,
-    earlier_ref,
-    hankel_ref,
-    center_ref,
-    scale_ref,
-    own_ref,
-    chunk_ref,
-):
-    rows = own_ref.shape[0]
-    steps = LANES // dims
-    packed_rows = rows // steps
-    tail_base = blocks * packed_rows
-    exclusion = M // 4
-    me = lax.axis_index("pb") * row_devices + lax.axis_index("row")
-
-    picks = lax.broadcasted_iota(jnp.int32, (LANES, steps * LANES), 0)
-    column = lax.broadcasted_iota(jnp.int32, (LANES, steps * LANES), 1)
-    pick = (picks == column // LANES * dims + column % dims).astype(jnp.float32)
-    pick = pick.astype(jnp.bfloat16)
-    pick = jnp.concatenate([pick, pick, pick], axis=0)
+    lax.fori_loop(1, blocks, arrive, 0, unroll=unroll)
 
     def later_steps(values, by):
         size = values.shape[0]
@@ -199,7 +182,7 @@
         scale = lax.rsqrt(square[:count] * (1.0 / M) + epsilon) * (1.0 / math.sqrt(M * dims))
         for values, ref in ((center, center_ref), (scale, scale_ref)):
             spread_out = jnp.dot(
-                three_terms(values), pick, preferred_element_type=jnp.float32
+                three_terms(values), pick_ref[...], preferred_element_type=jnp.float32
             )
             for step in range(steps):
                 ref[pl.ds(out + step, count, stride=steps), :] = spread_out[
@@ -237,14 +220,14 @@
         scores(me * rows + part * piece, own_ref, part * piece)
     own = own_ref[...]
     chunk_rows = chunk_ref.shape[0]
-    half = chunk_rows // 2
+    half = min(2 * rows, chunk_rows)
     offset = lax.broadcasted_iota(jnp.int32, (half, rows), 0) - lax.broadcasted_iota(
         jnp.int32, (half, rows), 1
     )
 
     def one_chunk(chunk, carry):
         later, earlier = carry
-        for side in range(2):
+        for side in range(chunk_rows // half):
             for part in range(half // piece):
                 row = side * half + part * piece
                 scores(chunk * chunk_rows + row, chunk_ref, row)
@@ -263,8 +246,25 @@
     chunk_blocks = chunk_rows // rows
     low = jnp.full((8, rows), -1.0, jnp.float32)
     later, earlier = lax.fori_loop(0, blocks // chunk_blocks, one_chunk, (low, low))
-    later_ref[...] = 2.0 - 2.0 * jnp.max(later, axis=0, keepdims=True)
-    earlier_ref[...] = 2.0 - 2.0 * jnp.max(earlier, axis=0, keepdims=True)
+    best_ref[pl.ds(0, 1), :] = 2.0 - 2.0 * jnp.max(later, axis=0, keepdims=True)
+    best_ref[pl.ds(1, 1), :] = 2.0 - 2.0 * jnp.max(earlier, axis=0, keepdims=True)
+
+    def sent(distance, carry):
+        block_copy(me, peer_of(distance), distance).wait_send()
+        return carry
+
+    lax.fori_loop(1, blocks, sent, 0, unroll=unroll)
+
+
+def split_kernel(best_ref, later_ref, earlier_ref, sems):
+    copies = [
+        pltpu.make_async_copy(best_ref.at[pl.ds(row, 1)], ref, sems.at[row])
+        for row, ref in enumerate((later_ref, earlier_ref))
+    ]
+    for copy in copies:
+        copy.start()
+    for copy in copies:
+        copy.wait()
 
 
 def per_device(record, record_tail, projection, window_start):
@@ -275,20 +275,27 @@
     blocks = lax.axis_size("pb") * row_devices
     steps = LANES // dims
     packed_rows = rows // steps
-    chunk_blocks = math.gcd(4, blocks)
+    chunk_blocks = math.gcd(16, blocks)
     vmem = pl.BlockSpec(memory_space=pltpu.VMEM)
     hbm = pl.BlockSpec(memory_space=pltpu.HBM)
     f32 = jnp.float32
-    packed = pl.pallas_call(
-        functools.partial(gather_kernel, blocks, row_devices),
-        out_shape=jax.ShapeDtypeStruct(((blocks + 1) * packed_rows + 2 * steps, LANES), f32),
-        in_specs=[hbm, hbm, hbm],
+    best = pl.pallas_call(
+        functools.partial(kernel, blocks, row_devices),
+        out_shape=jax.ShapeDtypeStruct((2, rows), f32),
+        in_specs=[pl.BlockSpec(memory_space=pltpu.SMEM), hbm, hbm, hbm],
         out_specs=vmem,
         scratch_shapes=[
             pltpu.VMEM((rows, channels), f32),
             pltpu.VMEM((head_rows, channels), f32),
             pltpu.VMEM((dims, channels), f32),
             pltpu.VMEM((rows, LANES), f32),
+            pltpu.VMEM(((blocks + 1) * packed_rows + 2 * steps, LANES), f32),
+            pltpu.VMEM(((blocks + 1) * rows, LANES), f32),
+            pltpu.VMEM(((blocks + 1) * rows, LANES), f32),
+            pltpu.VMEM(((blocks + 1) * rows, LANES), f32),
+            pltpu.VMEM((rows, M * dims), jnp.bfloat16),
+            pltpu.VMEM((chunk_blocks * rows, M * dims), jnp.bfloat16),
+            pltpu.VMEM((3 * LANES, steps * LANES), jnp.bfloat16),
             pltpu.SemaphoreType.DMA((2 + RECORD_COPIES,)),
             pltpu.SemaphoreType.DMA((blocks,)),
             pltpu.SemaphoreType.DMA((blocks,)),
@@ -296,19 +303,15 @@
         compiler_params=pltpu.CompilerParams(
             collective_id=0, has_side_effects=True, vmem_limit_bytes=62 * 1024 * 1024
         ),
-    )(record, record_tail, projection.T)
+    )(window_start, record, record_tail, projection.T)
     later, earlier = pl.pallas_call(
-        functools.partial(compute_kernel, blocks, row_devices, dims),
+        split_kernel,
         out_shape=[jax.ShapeDtypeStruct((1, rows), f32)] * 2,
-        in_specs=[pl.BlockSpec(memory_space=pltpu.SMEM), vmem],
-        out_specs=[vmem, vmem],
-        scratch_shapes=[pltpu.VMEM(((blocks + 1) * rows, LANES), f32)] * 3
-        + [
-            pltpu.VMEM((rows, M * dims), jnp.bfloat16),
-            pltpu.VMEM((chunk_blocks * rows, M * dims), jnp.bfloat16),
-        ],
-        compiler_params=pltpu.CompilerParams(vmem_limit_bytes=48 * 1024 * 1024),
-    )(window_start, packed)
+        in_specs=[hbm],
+        out_specs=[hbm, hbm],
+        scratch_shapes=[pltpu.SemaphoreType.DMA((2,))],
+        compiler_params=pltpu.CompilerParams(vmem_limit_bytes=62 * 1024 * 1024),
+    )(best)
     return later.reshape(rows), earlier.reshape(rows)
 
 

time: 17.3 us -> 16.6 us (0.960)
  local copies, waits for them, and re-layouts: 0.9 us -> 0 us
    unnamed x2 -> x0, local copies, waits for them, and re-layouts: 0.9 us -> none
    pallas_call x2, Pallas kernels: 15 us -> 15.1 us  [the longest x1 14 us: per_device(): pl.pallas_call(functools.partial(kernel, blocks, row_devices), out_shape=...]
where the time goes in v3:
time: 16.6 us; the launch traced here: 16.4 us
  Pallas kernels  15.1 us (91%)
  between operations  1.29 us (8%)
    pallas_call x1, Pallas kernels, per_device(): pl.pallas_call(functools.partial(kernel, blocks, row_devices), out_shape=...  14 us
    pallas_call x1, Pallas kernels, per_device(): pl.pallas_call(split_kernel, out_shape=[jax.ShapeDtypeStruct((1, rows), f...  1.15 us

profile of v3, /device:TPU:0, one launch (start us, length us, event | category | flops | bytes accessed | tf_op | source)
XLA Modules:
  0.0 16.4 jit_solution(14856737968191386453)
XLA Ops:
  1.3 14.0 %shard_map.59.best_ref = f32[2,128]{1,0:T(2,128)} custom-call(s32[1]{0:T(128)S(6)} %copy.6.start_ref, f32[128,1024]{1,0:T(8,128)} %record_hbm.1, f32[127,1024]{1,0:T(8,128)} %tail_hbm.1, f32[16,1024]{1,0:T(8,128)} %bitcast.3), custom_call_target="tpu_custom_call" | custom-call | tf_op jit(solution)/shard_map/pallas_call | solution.py:282
  15.3 1.2 %shard_map.60 = (f32[1,128]{1,0:T(1,128)}, f32[1,128]{1,0:T(1,128)}) custom-call(f32[2,128]{1,0:T(2,128)} %shard_map.59.best_ref), custom_call_target="tpu_custom_call" | custom-call | tf_op jit(solution)/shard_map/pallas_call | solution.py:307

commit v4 on v3

--- a/solution.py
+++ b/solution.py
@@ -12,7 +12,7 @@
 LANES = 128
 epsilon = 1e-05
 MESH = pl.DeviceIdType.MESH
-RECORD_COPIES = 4
+RECORD_COPIES = 8
 NT = (((1,), (1,)), ((), ()))
 
 
@@ -235,9 +235,9 @@
                 chunk_ref[pl.ds(side * half, half), :], own, NT,
                 preferred_element_type=jnp.float32,
             )
-            separation = offset + (chunk * chunk_rows + side * half - me * rows)
-            after = jnp.where(separation > exclusion, product, -1.0)
-            before = jnp.where(separation < -exclusion, product, -1.0)
+            origin = me * rows - chunk * chunk_rows - side * half
+            after = jnp.where(offset > origin + exclusion, product, -1.0)
+            before = jnp.where(offset < origin - exclusion, product, -1.0)
             after = jnp.max(after.reshape(half // 8, 8, rows), axis=0)
             before = jnp.max(before.reshape(half // 8, 8, rows), axis=0)
             later, earlier = jnp.maximum(later, after), jnp.maximum(earlier, before)

time: 16.6 us -> 16.5 us (level)
  no operation moved by 1% of the time
where the time goes in v4:
time: 16.5 us; the launch traced here: 16.3 us
  Pallas kernels  15 us (91%)
  between operations  1.29 us (8%)
    pallas_call x1, Pallas kernels, per_device(): pl.pallas_call(functools.partial(kernel, blocks, row_devices), out_shape=...  13.9 us
    pallas_call x1, Pallas kernels, per_device(): pl.pallas_call(split_kernel, out_shape=[jax.ShapeDtypeStruct((1, rows), f...  1.15 us

profile of v4, /device:TPU:0, one launch (start us, length us, event | category | flops | bytes accessed | tf_op | source)
XLA Modules:
  0.0 16.3 jit_solution(2071856426717868078)
XLA Ops:
  1.3 13.9 %shard_map.59.best_ref = f32[2,128]{1,0:T(2,128)} custom-call(s32[1]{0:T(128)S(6)} %copy.6.start_ref, f32[128,1024]{1,0:T(8,128)} %record_hbm.1, f32[127,1024]{1,0:T(8,128)} %tail_hbm.1, f32[16,1024]{1,0:T(8,128)} %bitcast.3), custom_call_target="tpu_custom_call" | custom-call | tf_op jit(solution)/shard_map/pallas_call | solution.py:282
  15.1 1.2 %shard_map.60 = (f32[1,128]{1,0:T(1,128)}, f32[1,128]{1,0:T(1,128)}) custom-call(f32[2,128]{1,0:T(2,128)} %shard_map.59.best_ref), custom_call_target="tpu_custom_call" | custom-call | tf_op jit(solution)/shard_map/pallas_call | solution.py:307
